TPU v7x, 32 devices: a whole 2x2x4 slice. The times are simulated.
32 devices in a mesh: groups: 2 (over x), expert: 8 (over z, y), tensor: 2 (over core).
Axes of the slice: x: 2, y: 2, z: 4, core: 2. Of those that a mesh axis runs over, the one named last changes fastest.
Arguments:
- tokens: bfloat16 [2048, 4096], P(('groups', 'expert', 'tensor')), parts along dimension 0, may hold values from -6 to 6
- expert_ids: int32 [2048, 8], P(('groups', 'expert', 'tensor')), parts along dimension 0, may hold values from 0 to 31, all different within a row; in each aligned block of 64 rows (0 to 63, 64 to 127, ...) at most 20 rows name the same one
- route_weights: float32 [2048, 8], P(('groups', 'expert', 'tensor')), parts along dimension 0, may hold values from 0.1 to 1
- gate_weight: bfloat16 [32, 768, 4096], P('expert', 'tensor'), may hold values from -0.09375 to 0.09375
- up_weight: bfloat16 [32, 768, 4096], P('expert', 'tensor'), may hold values from -0.09375 to 0.09375
- down_weight: bfloat16 [32, 768, 4096], P('expert', 'tensor'), may hold values from -0.21875 to 0.21875
Outputs:
- combined: bfloat16 [2048, 4096], P(('groups', 'expert', 'tensor')), parts along dimension 0
There are 2 independent parts, one for each index of `groups`. A program takes and returns all parts, laid end to end along the dimension named above; an argument that names none is the same for every part. Nothing has to cross between parts.
Inputs may be any that keep to these rules, and one draw needn't show every extreme that they name: `expert_ids`: each token names 8 different experts. Within each aligned block of 64 tokens no expert is named by more than 20 tokens, a bound that some block reaches.
All inputs are finite; a program needn't handle non-finite values.
Results may differ from a plain program's by a relative error of at most 0.008.
Values may be sent and summed in bfloat16 or wider, within the bound.
A program may use at most 192 MiB of HBM per device.

v0:
```python
import jax
import jax.numpy as jnp
from jax import lax
from jax.sharding import PartitionSpec as P

EXPERTS = 32
CAP = 20


def expert_rows(row_block, gate_part, up_part, down_part):
    gate_value = jnp.einsum(
        "erd,efd->erf", row_block, gate_part, preferred_element_type=jnp.float32
    )
    up_value = jnp.einsum("erd,efd->erf", row_block, up_part, preferred_element_type=jnp.float32)
    hidden = (jax.nn.silu(gate_value) * up_value).astype(jnp.bfloat16)
    return jnp.einsum("erf,efd->erd", hidden, down_part, preferred_element_type=jnp.float32)


def shards(tokens, expert_ids, route_weights, gate_weight, up_weight, down_weight):
    labels = jnp.arange(EXPERTS, dtype=jnp.int32)
    chosen = jnp.sum((expert_ids[:, :, None] == labels[None, None, :]).astype(jnp.int32), axis=1)
    before = jnp.cumsum(chosen, axis=0) - chosen
    slot_rank = jnp.take_along_axis(before, expert_ids, axis=1)
    slot_index = expert_ids * CAP + slot_rank
    places = jnp.arange(EXPERTS * CAP, dtype=jnp.int32)
    dispatch_table = jnp.any(places[:, None, None] == slot_index[None, :, :], axis=2).astype(
        jnp.bfloat16
    )
    packed = jnp.dot(dispatch_table, tokens, preferred_element_type=jnp.float32).astype(
        jnp.bfloat16
    )
    packed = packed.reshape(EXPERTS, CAP, tokens.shape[1])
    arrived = lax.all_to_all(packed, "expert", split_axis=0, concat_axis=1, tiled=True)
    partial_value = expert_rows(
        lax.all_gather(arrived, "tensor", axis=1, tiled=True), gate_weight, up_weight, down_weight
    )
    summed = lax.psum_scatter(partial_value, "tensor", scatter_dimension=1, tiled=True)
    results = summed.astype(jnp.bfloat16)
    returned = lax.all_to_all(results, "expert", split_axis=1, concat_axis=0, tiled=True)
    flat_rows = returned.reshape(EXPERTS * CAP, returned.shape[2])
    picked = jnp.take(flat_rows, slot_index, axis=0)
    combined = jnp.einsum("tk,tkd->td", route_weights, picked.astype(jnp.float32))
    return combined.astype(jnp.bfloat16)


def solution(mesh):
    placed = (
        P(("groups", "expert", "tensor"), None),
        P(("groups", "expert", "tensor"), None),
        P(("groups", "expert", "tensor"), None),
        P("expert", "tensor", None),
        P("expert", "tensor", None),
        P("expert", "tensor", None),
    )
    return jax.shard_map(
        shards,
        mesh=mesh,
        in_specs=placed,
        out_specs=P(("groups", "expert", "tensor"), None),
        check_vma=False,
    )
```

profile of v0, /device:TPU:0, one launch (start us, length us, event | category | flops | bytes accessed | tf_op | source)
XLA Modules:
  0.0 442.4 jit_solution(3010310972378820107)
XLA Ops:
  6.5 0.8 convert_reduce_fusion
  7.3 0.7 bitcast_or_fusion
  8.1 0.1 reduce_window_sum.11
  8.2 0.1 copy.51
  8.3 0.1 reshape.34
  8.4 3.8 gather_fusion.1
  12.2 0.1 reshape.37
  12.3 0.1 copy.54
  12.4 0.5 fusion.4
  12.9 4.0 convolution_convert_fusion
  16.9 7.7 %reshape.24 = bf16[32,20,4096]{2,1,0:T(8,128)(2,1)} reshape(bf16[640,4096]{1,0:T(8,128)(2,1)} %convolution_convert_fusion) | data formatting | bytes 10485760 | tf_op jit(solution)/shard_map/reshape | solution.py:32
  24.5 145.4 %all_to_all.33 = bf16[32,20,4096]{2,1,0:T(8,128)(2,1)S(1)} all-to-all(bf16[32,20,4096]{2,1,0:T(8,128)(2,1)} %reshape.24), channel_id=1, replica_groups=mesh['groups'=2,'expert'=8,'tensor'=2] {'expert'}, dimensions={0} | all-to-all | bytes 10485760 | tf_op jit(solution)/shard_map/all_to_all | solution.py:33
  169.9 4.1 copy.55
  174.1 5.2 %copy.56 = bf16[4,160,4096]{2,1,0:T(8,128)(2,1)} copy(bf16[4,160,4096]{2,0,1:T(4,128)(2,1)S(1)} %bitcast.27) | data formatting | bytes 10485760 | tf_op jit(solution)/shard_map/all_to_all | solution.py:33
  179.3 0.2 reduce-scatter.2.cloned.1.call-start
  179.5 21.5 %all-gather.2.cloned.1.call-done = bf16[4,320,4096]{2,1,0:T(8,128)(2,1)} async-done(((bf16[4,160,4096]{2,1,0:T(8,128)(2,1)}), bf16[4,320,4096]{2,1,0:T(8,128)(2,1)}) %all-gather.2.cloned.1.call-update) | async-done | bytes 10485776 | tf_op jit(solution)/shard_map/all_gather | solution.py:35
  201.0 14.2 %fusion.8 = f32[4,320,384]{2,1,0:T(8,128)S(1)} fusion(bf16[4,320,4096]{2,1,0:T(8,128)(2,1)} %all-gather.2.cloned.1.call-done, bf16[4,384,4096]{2,1,0:T(8,128)(2,1)} %param.9), kind=kOutput, calls=%fused_computation.23 | convolution fusion | flops 4026531840 | bytes 25034752 | tf_op jit(solution)/shard_map/erd,efd->erf/dot_general | solution.py:11
  215.2 22.3 %fusion.3 = f32[4,320,4096]{2,1,0:T(8,128)} fusion(bf16[4,384,4096]{2,1,0:T(8,128)(2,1)} %param.11, f32[4,320,384]{2,1,0:T(8,128)S(1)} %fusion.8, bf16[4,320,4096]{2,1,0:T(8,128)(2,1)} %all-gather.2.cloned.1.call-done, bf16[4,384,4096]{2,1,0:T(8,128)(2,1)} %param.10), kind=kOutput, calls=%fused_computation.8 | convolution fusion | flops 8056012800 | bytes 58589184 | tf_op jit(solution)/shard_map/erf,efd->erd/dot_general | solution.py:16
  237.5 32.0 %reduce-scatter.2.cloned.1.call-done = f32[4,160,4096]{2,1,0:T(8,128)} async-done(((f32[4,320,4096]{2,1,0:T(8,128)}), f32[4,160,4096]{2,1,0:T(8,128)}) %reduce-scatter.2.cloned.1.call-update) | async-done | bytes 10485776 | tf_op jit(solution)/shard_map/reduce_scatter | solution.py:37
  269.5 4.8 %convert_element_type.20 = bf16[4,160,4096]{2,1,0:T(8,128)(2,1)S(1)} convert(f32[4,160,4096]{2,1,0:T(8,128)} %reduce-scatter.2.cloned.1.call-done) | non-fusion elementwise | flops 2621440 | bytes 15728640 | tf_op jit(solution)/shard_map/convert_element_type | solution.py:38
  274.2 6.3 %copy.57 = bf16[4,160,4096]{2,0,1:T(4,128)(2,1)} copy(bf16[4,160,4096]{2,1,0:T(8,128)(2,1)S(1)} %convert_element_type.20) | data formatting | bytes 10485760 | tf_op jit(solution)/shard_map/convert_element_type | solution.py:38
  280.6 6.0 %all-to-all-start.1 = ((bf16[4,160,4096]{2,0,1:T(4,128)(2,1)}), bf16[4,160,4096]{2,0,1:T(4,128)(2,1)}, u32[]{:S(2)}, u32[]{:S(2)}) async-start(bf16[4,160,4096]{2,0,1:T(4,128)(2,1)} %copy.57), calls=%async_computation.2 | async-start | bytes 10485760 | tf_op jit(solution)/shard_map/all_to_all | solution.py:39
  286.6 0.1 copy.59
  286.7 0.1 reshape.28
  286.8 0.1 copy.53
  286.9 0.1 copy.60
  287.0 115.7 %all-to-all-done.1 = bf16[4,160,4096]{2,0,1:T(4,128)(2,1)} async-done(((bf16[4,160,4096]{2,0,1:T(4,128)(2,1)}), bf16[4,160,4096]{2,0,1:T(4,128)(2,1)}, u32[]{:S(2)}, u32[]{:S(2)}) %all-to-all-start.1) | async-done | bytes 5242912 | tf_op jit(solution)/shard_map/all_to_all | solution.py:39
  402.7 8.4 %copy.58 = bf16[8,4,20,4096]{3,2,1,0:T(8,128)(2,1)} copy(bf16[8,4,20,4096]{3,1,2,0:T(4,128)(2,1)} %bitcast.5) | data formatting | bytes 10485760 | tf_op jit(solution)/shard_map/all_to_all | solution.py:39
  411.1 7.8 %reshape.25 = bf16[640,4096]{1,0:T(8,128)(2,1)} reshape(bf16[8,4,20,4096]{3,2,1,0:T(8,128)(2,1)} %copy.58) | data formatting | bytes 10485760 | tf_op jit(solution)/shard_map/reshape | solution.py:40
  418.9 11.8 %gather_fusion = bf16[512,4096]{1,0:T(8,128)(2,1)} fusion(bf16[640,4096]{1,0:T(8,128)(2,1)} %reshape.25, s32[1024]{0:T(1024)S(1)} %pad_clamp_fusion), kind=kCustom, calls=%fused_computation | custom fusion | bytes 8390656 | tf_op jit(solution)/shard_map/jit(_take)/gather | solution.py:41
  430.7 3.5 fusion
  434.2 1.4 copy.63
  (17 shorter events, 0.2 us)
Async XLA Ops:
  6.5 6.4 %copy-start = (bf16[64,4096]{1,0:T(8,128)(2,1)S(1)}, bf16[64,4096]{1,0:T(8,128)(2,1)}, u32[]{:S(2)}) copy-start(bf16[64,4096]{1,0:T(8,128)(2,1)} %param.6) | copy-start | bytes 1572868
  6.5 194.4 %all-gather.2.cloned.1.call-start = ((), (), s32[]{:S(2)}) async-start(), calls=%async_computation.3 | async-start | bytes 15728640 | tf_op jit(solution)/shard_map/all_gather | solution.py:35
  8.4 3.9 copy-start.2
  179.3 90.2 %reduce-scatter.2.cloned.1.call-start = ((), (), s32[]{:S(2)}) async-start(), calls=%async_computation.4 | async-start | bytes 31457280 | tf_op jit(solution)/shard_map/reduce_scatter | solution.py:37
  280.6 6.3 %copy-start.3 = (f32[64,8]{0,1:T(8,128)S(1)}, f32[64,8]{0,1:T(8,128)}, u32[]{:S(2)}) copy-start(f32[64,8]{0,1:T(8,128)} %param.8) | copy-start | bytes 6148
  280.6 122.1 %all-to-all-start.1 = ((bf16[4,160,4096]{2,0,1:T(4,128)(2,1)}), bf16[4,160,4096]{2,0,1:T(4,128)(2,1)}, u32[]{:S(2)}, u32[]{:S(2)}) async-start(bf16[4,160,4096]{2,0,1:T(4,128)(2,1)} %copy.57), calls=%async_computation.2 | async-start | bytes 10485760 | tf_op jit(solution)/shard_map/all_to_all | solution.py:39
  418.9 16.7 %copy-start.1 = (bf16[64,4096]{1,0:T(8,128)(2,1)S(1)}, bf16[64,4096]{1,0:T(8,128)(2,1)}, u32[]{:S(2)}) copy-start(bf16[64,4096]{1,0:T(8,128)(2,1)} %param.6) | copy-start | bytes 1572868
Sparse Core Ops, SparseCore 0:
  179.4 21.5 all-gather.1
  237.6 31.8 reduce-scatter.1
where the time goes:
time: 443 us; the launch traced here: 442 us
  waiting for transfers between devices  169 us (38%)
  blocking collectives  145 us (33%)
  local copies, waits for them, and re-layouts  57.3 us (13%)
  matrix products  44 us (10%)
  between operations  13.5 us (3%)
  other arithmetic  6.81 us (2%)
  starting transfers between devices  6.21 us (1%)
    all_to_all x1, blocking collectives, shards(): lax.all_to_all(packed, 'expert', split_axis=0, concat_axis=1, tiled=True)  145 us
    all_to_all x1, waiting for transfers between devices, shards(): lax.all_to_all(results, 'expert', split_axis=1, concat_axis=0, tiled=True)  116 us
    reduce_scatter x1, waiting for transfers between devices, shards(): lax.psum_scatter(partial_value, 'tensor', scatter_dimension=1, tiled=True)  32 us
    dot_general x1, matrix products, expert_rows(): jnp.einsum('erf,efd->erd', hidden, down_part, preferred_element_type=jnp....  22.3 us
    all_gather x1, waiting for transfers between devices, shards(): lax.all_gather(arrived, 'tensor', axis=1, tiled=True)  21.5 us
    dot_general x1, matrix products, expert_rows(): jnp.einsum('erd,efd->erf', row_block, gate_part, preferred_element_type=j...  14.2 us
    gather x1, local copies, waits for them, and re-layouts, shards(): picked = jnp.take(flat_rows, slot_index, axis=0)  11.8 us
    all_to_all x2, local copies, waits for them, and re-layouts, shards(): lax.all_to_all(packed, 'expert', split_axis=0, concat_axis=1, tiled=True)  9.28 us
  transfers between devices with their start and end apart: 3, of which 3 were waited for; matrix products, arithmetic and copies ran while one was open for 0% of the time, Pallas kernels for 0%

commit v1 on v0

v1 whole, which is shorter than its diff:
```python
import functools

import jax
import jax.numpy as jnp
from jax import lax
from jax.experimental import pallas as pl
from jax.experimental.pallas import tpu as pltpu
from jax.sharding import PartitionSpec as P

MESH = pl.DeviceIdType.MESH
EXTRA = 128
HID_TILE = 256
OUT_TILE = 512


def nearest(z, step):
    lower = 1 - z // 2
    edge = z * lower + (3 - z) * (1 - lower)
    near = step + edge * (1 - step // 2) * (1 - 2 * (step % 2))
    return near * lower + (3 - near) * (1 - lower)


def kernel(
    line, held, tokens_ref, ids_ref, route_ref, gate_ref, up_ref, down_ref, out_ref,
    tok, gate, up, down, hid, part, from_core, from_y, from_z,
    weight_sem, own_sem, zs, zr, ys, yr, cs, cr, pcs, pcr, pys, pyr, pzs, pzr,
):
    place, c = lax.axis_index("expert"), lax.axis_index("tensor")
    z, y = place // 2, place % 2
    rows, width = tokens_ref.shape
    units = gate_ref.shape[0]
    each = units // held
    to_core = {"tensor": 1 - c}
    to_y = {"expert": z * 2 + 1 - y}

    def remote(src, dst, send, recv, device):
        return pltpu.make_async_remote_copy(
            src_ref=src, dst_ref=dst, send_sem=send, recv_sem=recv,
            device_id=device, device_id_type=MESH,
        )

    barrier = pltpu.get_barrier_semaphore()
    pl.semaphore_signal(barrier, inc=1, device_id=to_core, device_id_type=MESH)
    pl.semaphore_signal(barrier, inc=1, device_id=to_y, device_id_type=MESH)
    for d in range(1, line):
        pl.semaphore_signal(
            barrier, inc=1, device_id={"expert": nearest(z, d) * 2 + y}, device_id_type=MESH
        )

    own = pltpu.make_async_copy(tokens_ref, tok.at[z, c, y, :, pl.ds(0, width)], own_sem)
    own.start()
    loads = []
    half = units // 2
    for number, (src, dst) in enumerate(((gate_ref, gate), (up_ref, up), (down_ref, down))):
        loads.append(pltpu.make_async_copy(src, dst, weight_sem.at[number]))
        loads[-1].start()

    lane = lax.broadcasted_iota(jnp.int32, (rows, EXTRA), 1)
    dense = jnp.zeros((rows, EXTRA), jnp.float32)
    for k in range(ids_ref.shape[1]):
        dense += jnp.where(ids_ref[:, k : k + 1] == lane % 32, route_ref[:, k : k + 1], 0.0)
    high = dense.astype(jnp.bfloat16).astype(jnp.float32)
    middle = (dense - high).astype(jnp.bfloat16).astype(jnp.float32)
    low = dense - high - middle
    terms = jnp.where(lane < 32, high, jnp.where(lane < 64, middle, low))
    tok[z, c, y, :, pl.ds(width, EXTRA)] = terms.astype(jnp.bfloat16)
    own.wait()
    pl.semaphore_wait(barrier, line + 1)

    def z_send(d):
        block = tok.at[z, c, y]
        return remote(block, block, zs.at[d], zr.at[z], {"expert": nearest(z, d) * 2 + y})

    def z_arrival(at):
        block = tok.at[at, c, y]
        return remote(block, block, zs.at[0], zr.at[at], to_y)

    def y_send(at):
        block = tok.at[at, c, y]
        return remote(block, block, ys.at[at], yr.at[at], to_y)

    def y_arrival(at):
        block = tok.at[at, c, 1 - y]
        return remote(block, block, ys.at[at], yr.at[at], to_y)

    def c_send(at, row):
        block = tok.at[at, c, row]
        return remote(block, block, cs.at[at, row], cr.at[at, row], to_core)

    def c_arrival(at, row):
        block = tok.at[at, 1 - c, row]
        return remote(block, block, cs.at[at, row], cr.at[at, row], to_core)

    y_send(z).start()
    for d in range(1, line):
        z_send(d).start()
    c_send(z, y).start()

    def arrive_first(step):
        at = nearest(z, step)
        z_arrival(at).wait_recv()
        y_send(at).start()
        c_send(at, y).start()

    def arrive_second(step):
        at = nearest(z, step)
        y_arrival(at).wait_recv()
        c_send(at, 1 - y).start()
        c_arrival(at, y).wait_recv()
        c_arrival(at, 1 - y).wait_recv()

    def part_core(step):
        at = nearest(z, step)
        return remote(
            part.at[step % 2, 1 - c], from_core.at[at], pcs.at[step], pcr.at[step], to_core
        )

    def part_y(step):
        at = nearest(z, step)
        return remote(
            part.at[step % 2, c, 1 - y], from_y.at[at], pys.at[step], pyr.at[step], to_y
        )

    def part_z(step):
        at = nearest(z, step)
        return remote(
            from_y.at[at], from_z.at[z], pzs.at[step], pzr.at[z], {"expert": at * 2 + y}
        )

    def add_core(step):
        at = nearest(z, step)
        part_core(step).wait_recv()
        for row in range(2):
            mine = part[step % 2, c, row].astype(jnp.float32)
            part[step % 2, c, row] = (mine + from_core[at, row].astype(jnp.float32)).astype(
                jnp.bfloat16
            )
        part_y(step).start()

    def add_y(step):
        at = nearest(z, step)
        part_y(step).wait_recv()
        mine = part[step % 2, c, y].astype(jnp.float32)
        from_y[at] = (mine + from_y[at].astype(jnp.float32)).astype(jnp.bfloat16)

        @pl.when(step > 0)
        def _():
            part_z(step).start()

    first = place * held

    def work(step, carry):
        at = nearest(z, step)

        @pl.when(step < line - 1)
        def _():
            arrive_first(step + 1)

        arrive_second(step)

        @pl.when(step == 0)
        def _():
            loads[0].wait()
            loads[1].wait()

        def hidden_tile(j, carry):
            start = pl.multiple_of(j * HID_TILE, HID_TILE)
            x = tok[at, :, :, :, pl.ds(0, width)].reshape(4 * rows, width)
            terms = tok[at, :, :, :, pl.ds(width, EXTRA)].reshape(4 * rows, EXTRA)
            transposed = (((1,), (1,)), ((), ()))
            g = lax.dot_general(
                x, gate[pl.ds(start, HID_TILE), :], transposed,
                preferred_element_type=jnp.float32,
            )
            u = lax.dot_general(
                x, up[pl.ds(start, HID_TILE), :], transposed,
                preferred_element_type=jnp.float32,
            )
            source = lax.broadcasted_iota(jnp.int32, (EXTRA, HID_TILE), 0)
            unit = start + lax.broadcasted_iota(jnp.int32, (EXTRA, HID_TILE), 1)
            expert = first
            for e in range(1, held):
                expert = expert + (unit >= e * each).astype(jnp.int32)
            chosen = jnp.where((source % 32 == expert) & (source < 96), 1.0, 0.0)
            weight = jnp.dot(
                terms, chosen.astype(jnp.bfloat16), preferred_element_type=jnp.float32
            )
            value = g / (1.0 + jnp.exp(-g)) * u * weight
            hid[:, pl.ds(start, HID_TILE)] = value.astype(jnp.bfloat16)
            return carry

        lax.fori_loop(0, units // HID_TILE, hidden_tile, 0)

        @pl.when(step > 0)
        def _():
            add_core(step - 1)

        @pl.when(step == 0)
        def _():
            loads[2].wait()

        @pl.when(step > 1)
        def _():
            part_core(step - 2).wait_send()
            part_y(step - 2).wait_send()

        def out_tile(j, carry):
            cols = pl.ds(pl.multiple_of(j * OUT_TILE, OUT_TILE), OUT_TILE)
            total = jnp.dot(hid[...], down[:, cols], preferred_element_type=jnp.float32)
            part[step % 2, :, :, :, cols] = total.astype(jnp.bfloat16).reshape(
                2, 2, rows, OUT_TILE
            )
            return carry

        lax.fori_loop(0, width // OUT_TILE, out_tile, 0)
        part_core(step).start()

        @pl.when(step > 0)
        def _():
            add_y(step - 1)

        return carry

    lax.fori_loop(0, line, work, 0)
    add_core(line - 1)
    add_y(line - 1)

    total = from_y[z].astype(jnp.float32)
    for d in range(1, line):
        at = nearest(z, d)
        remote(from_y.at[at], from_z.at[at], pzs.at[d], pzr.at[at], to_y).wait_recv()
        total += from_z[at].astype(jnp.float32)
    out_ref[...] = total.astype(out_ref.dtype)

    for d in range(1, line):
        z_send(d).wait_send()
        part_z(d).wait_send()
    for at in range(line):
        y_send(at).wait_send()
        for row in range(2):
            c_send(at, row).wait_send()
    for step in range(line - 2, line):
        part_core(step).wait_send()
        part_y(step).wait_send()


def in_one_kernel(tokens, expert_ids, route_weights, gate_weight, up_weight, down_weight):
    rows, width = tokens.shape
    line = lax.axis_size("expert") // 2
    held, each, _ = gate_weight.shape
    units = held * each
    bf16 = jnp.bfloat16
    dma = pltpu.SemaphoreType.DMA
    vmem = pl.BlockSpec(memory_space=pltpu.VMEM)
    hbm = pl.BlockSpec(memory_space=pl.ANY)
    flat = (units, width)
    group_rows = line * 4 * rows
    return pl.pallas_call(
        functools.partial(kernel, line, held),
        out_shape=jax.ShapeDtypeStruct((rows, width), bf16),
        in_specs=[hbm, vmem, vmem, hbm, hbm, hbm],
        out_specs=vmem,
        scratch_shapes=[
            pltpu.VMEM((line, 2, 2, rows, width + EXTRA), bf16),
            pltpu.VMEM(flat, bf16),
            pltpu.VMEM(flat, bf16),
            pltpu.VMEM(flat, bf16),
            pltpu.VMEM((4 * rows, units), bf16),
            pltpu.VMEM((2, 2, 2, rows, width), bf16),
            pltpu.VMEM((line, 2, rows, width), bf16),
            pltpu.VMEM((line, rows, width), bf16),
            pltpu.VMEM((line, rows, width), bf16),
            dma((3,)),
            dma,
            dma((line,)),
            dma((line,)),
            dma((line,)),
            dma((line,)),
            dma((line, 2)),
            dma((line, 2)),
            dma((line,)),
            dma((line,)),
            dma((line,)),
            dma((line,)),
            dma((line,)),
            dma((line,)),
        ],
        compiler_params=pltpu.CompilerParams(
            collective_id=0, has_side_effects=True, vmem_limit_bytes=63 * 1024 * 1024
        ),
        cost_estimate=pl.CostEstimate(
            flops=6 * group_rows * units * width,
            bytes_accessed=6 * units * width,
            transcendentals=group_rows * units,
        ),
        name="experts",
    )(
        tokens, expert_ids, route_weights,
        gate_weight.reshape(flat), up_weight.reshape(flat), down_weight.reshape(flat),
    )


def in_steps(tokens, expert_ids, route_weights, gate_weight, up_weight, down_weight):
    held = gate_weight.shape[0]
    experts = held * lax.axis_size("expert")
    labels = jnp.arange(experts, dtype=jnp.int32)
    named = expert_ids[:, :, None] == labels[None, None, :]
    weights = jnp.sum(jnp.where(named, route_weights[:, :, None], 0.0), axis=1)
    group = ("expert", "tensor")
    rows = lax.all_gather(tokens, group, axis=0, tiled=True)
    all_weights = lax.all_gather(weights, group, axis=0, tiled=True)
    first = lax.axis_index("expert") * held
    mine = lax.dynamic_slice_in_dim(all_weights, first, held, axis=1)
    total, hidden_units = rows.shape[0], gate_weight.shape[1]
    flat = (held * hidden_units, gate_weight.shape[2])
    transposed = (((1,), (1,)), ((), ()))
    gate = lax.dot_general(
        rows, gate_weight.reshape(flat), transposed, preferred_element_type=jnp.float32
    )
    up = lax.dot_general(
        rows, up_weight.reshape(flat), transposed, preferred_element_type=jnp.float32
    )
    scaled = (jax.nn.silu(gate) * up).reshape(total, held, hidden_units) * mine[:, :, None]
    hidden = scaled.reshape(total, held * hidden_units).astype(jnp.bfloat16)
    partial = jnp.dot(hidden, down_weight.reshape(flat), preferred_element_type=jnp.float32)
    return lax.psum_scatter(
        partial.astype(jnp.bfloat16), group, scatter_dimension=0, tiled=True
    )


def solution(mesh):
    spread = P(("groups", "expert", "tensor"), None)
    weight = P("expert", "tensor", None)
    small = mesh.shape["expert"] == 8 and mesh.shape["tensor"] == 2
    return jax.shard_map(
        in_one_kernel if small else in_steps,
        mesh=mesh,
        in_specs=(spread,) * 3 + (weight,) * 3,
        out_specs=spread,
        check_vma=False,
    )
```

time: 443 us -> 167 us (0.38)
  waiting for transfers between devices: 169 us -> 0 us
  Pallas kernels: 0 us -> 162 us
  blocking collectives: 145 us -> 0 us
  local copies, waits for them, and re-layouts: 57.3 us -> 4.62 us
  matrix products: 44 us -> 0 us
  between operations: 13.5 us -> 0.01 us
  other arithmetic: 6.81 us -> 0 us
  starting transfers between devices: 6.21 us -> 0 us
    pallas_call x0 -> x1, Pallas kernels: none -> 162 us  [in_one_kernel(): pl.pallas_call(functools.partial(kernel, line, held), out_shape=jax.Shape...]
    all_to_all x1 -> x0, blocking collectives: 145 us -> none  [shards(): lax.all_to_all(packed, 'expert', split_axis=0, concat_axis=1, tiled=True)]
    all_to_all x1 -> x0, waiting for transfers between devices: 116 us -> none  [shards(): lax.all_to_all(results, 'expert', split_axis=1, concat_axis=0, tiled=True)]
    dot_general x4 -> x0, matrix products: 44 us -> none  [the longest x1 22.3 us: expert_rows(): jnp.einsum('erf,efd->erd', hidden, down_part, preferred_element_type=jnp....]
    reduce_scatter x1 -> x0, waiting for transfers between devices: 32 us -> none  [shards(): lax.psum_scatter(partial_value, 'tensor', scatter_dimension=1, tiled=True)]
    all_gather x1 -> x0, waiting for transfers between devices: 21.5 us -> none  [shards(): lax.all_gather(arrived, 'tensor', axis=1, tiled=True)]
    all_to_all x3 -> x0, local copies, waits for them, and re-layouts: 17.6 us -> none  [the longest x2 9.28 us: shards(): lax.all_to_all(packed, 'expert', split_axis=0, concat_axis=1, tiled=True)]
    gather x6 -> x0, local copies, waits for them, and re-layouts: 15.9 us -> none  [the longest x1 11.8 us: shards(): picked = jnp.take(flat_rows, slot_index, axis=0)]
  transfers between devices with their start and end apart: 3 -> 0, of which waited for: 3 -> 0; matrix products, arithmetic and copies ran while one was open for 0% -> 0% of each run, Pallas kernels for 0% -> 0%
where the time goes in v1:
time: 167 us
  Pallas kernels  162 us (97%)
  local copies, waits for them, and re-layouts  4.62 us (3%)
    pallas_call x1, Pallas kernels, in_one_kernel(): pl.pallas_call(functools.partial(kernel, line, held), out_shape=jax.Shape...  162 us
    unnamed x3, local copies, waits for them, and re-layouts  4.62 us

profile of v1, /device:TPU:0, one launch (start us, length us, event | category | flops | bytes accessed | tf_op | source)
XLA Modules:
  0.0 166.8 jit_solution(167369741795135001)
XLA Ops:
  0.0 1.4 copy.7.ids_ref
  1.4 1.4 copy.8.route_ref
  2.8 162.2 %experts.1 = bf16[64,4096]{1,0:T(8,128)(2,1)} custom-call(bf16[64,4096]{1,0:T(8,128)(2,1)} %tokens_ref.1, s32[64,8]{1,0:T(8,128)} %copy.7.ids_ref, f32[64,8]{1,0:T(8,128)} %copy.8.route_ref, bf16[1536,4096]{1,0:T(8,128)(2,1)} %bitcast.3, bf16[1536,4096]{1,0:T(8,128)(2,1)} %bitcast.4, bf16[1536,4096]{1,0:T(8,128)(2,1)} %bitcast.5), custom_call_target="tpu_custom_call" | custom-call | flops 38654705664 | bytes 37748736 | tf_op jit(solution)/shard_map/experts/pallas_call | solution.py:258
  165.0 1.9 %copy.10 = bf16[64,4096]{1,0:T(8,128)(2,1)} copy(bf16[64,4096]{1,0:T(8,128)(2,1)} %experts.1) | data formatting | bytes 1048576

commit v2 on v1

--- a/solution.py
+++ b/solution.py
@@ -11,6 +11,7 @@
 EXTRA = 128
 HID_TILE = 256
 OUT_TILE = 512
+HALVES = 2
 
 
 def nearest(z, step):
@@ -18,6 +19,10 @@
     edge = z * lower + (3 - z) * (1 - lower)
     near = step + edge * (1 - step // 2) * (1 - 2 * (step % 2))
     return near * lower + (3 - near) * (1 - lower)
+
+
+def slot(step):
+    return step - 2 * (step // 3)
 
 
 def kernel(
@@ -50,7 +55,6 @@
     own = pltpu.make_async_copy(tokens_ref, tok.at[z, c, y, :, pl.ds(0, width)], own_sem)
     own.start()
     loads = []
-    half = units // 2
     for number, (src, dst) in enumerate(((gate_ref, gate), (up_ref, up), (down_ref, down))):
         loads.append(pltpu.make_async_copy(src, dst, weight_sem.at[number]))
         loads[-1].start()
@@ -67,13 +71,15 @@
     own.wait()
     pl.semaphore_wait(barrier, line + 1)
 
-    def z_send(d):
-        block = tok.at[z, c, y]
-        return remote(block, block, zs.at[d], zr.at[z], {"expert": nearest(z, d) * 2 + y})
+    def z_hop(at, up_line):
+        block = tok.at[at, c, y]
+        side = 1 if up_line else 0
+        there = (z + 2 * side - 1) * 2 + y
+        return remote(block, block, zs.at[at, side], zr.at[at], {"expert": there})
 
     def z_arrival(at):
         block = tok.at[at, c, y]
-        return remote(block, block, zs.at[0], zr.at[at], to_y)
+        return remote(block, block, zs.at[at, 0], zr.at[at], to_y)
 
     def y_send(at):
         block = tok.at[at, c, y]
@@ -91,72 +97,93 @@
         block = tok.at[at, 1 - c, row]
         return remote(block, block, cs.at[at, row], cr.at[at, row], to_core)
 
+    @pl.when(z < line - 1)
+    def _():
+        z_hop(z, True).start()
+
+    @pl.when(z > 0)
+    def _():
+        z_hop(z, False).start()
+
     y_send(z).start()
-    for d in range(1, line):
-        z_send(d).start()
     c_send(z, y).start()
 
-    def arrive_first(step):
-        at = nearest(z, step)
-        z_arrival(at).wait_recv()
-        y_send(at).start()
-        c_send(at, y).start()
-
-    def arrive_second(step):
+    def chain(far):
+        @pl.when(z >= far)
+        def _():
+            at = z - far
+            z_arrival(at).wait_recv()
+
+            @pl.when(z < line - 1)
+            def _():
+                z_hop(at, True).start()
+
+            y_send(at).start()
+            c_send(at, y).start()
+
+        @pl.when(z + far < line)
+        def _():
+            at = z + far
+            z_arrival(at).wait_recv()
+
+            @pl.when(z > 0)
+            def _():
+                z_hop(at, False).start()
+
+            y_send(at).start()
+            c_send(at, y).start()
+
+    def arrive(step):
         at = nearest(z, step)
         y_arrival(at).wait_recv()
         c_send(at, 1 - y).start()
         c_arrival(at, y).wait_recv()
         c_arrival(at, 1 - y).wait_recv()
 
-    def part_core(step):
+    def part_core(step, h):
         at = nearest(z, step)
         return remote(
-            part.at[step % 2, 1 - c], from_core.at[at], pcs.at[step], pcr.at[step], to_core
-        )
-
-    def part_y(step):
+            part.at[slot(step), h, 1 - c], from_core.at[at, h],
+            pcs.at[step, h], pcr.at[step, h], to_core,
+        )
+
+    def part_y(step, h):
         at = nearest(z, step)
         return remote(
-            part.at[step % 2, c, 1 - y], from_y.at[at], pys.at[step], pyr.at[step], to_y
-        )
-
-    def part_z(step):
+            part.at[slot(step), h, c, 1 - y], from_y.at[at, h],
+            pys.at[step, h], pyr.at[step, h], to_y,
+        )
+
+    def part_z(step, h):
         at = nearest(z, step)
         return remote(
-            from_y.at[at], from_z.at[z], pzs.at[step], pzr.at[z], {"expert": at * 2 + y}
-        )
-
-    def add_core(step):
-        at = nearest(z, step)
-        part_core(step).wait_recv()
-        for row in range(2):
-            mine = part[step % 2, c, row].astype(jnp.float32)
-            part[step % 2, c, row] = (mine + from_core[at, row].astype(jnp.float32)).astype(
-                jnp.bfloat16
-            )
-        part_y(step).start()
-
-    def add_y(step):
-        at = nearest(z, step)
-        part_y(step).wait_recv()
-        mine = part[step % 2, c, y].astype(jnp.float32)
-        from_y[at] = (mine + from_y[at].astype(jnp.float32)).astype(jnp.bfloat16)
-
-        @pl.when(step > 0)
-        def _():
-            part_z(step).start()
+            from_y.at[at, h], from_z.at[z, h],
+            pzs.at[step, h], pzr.at[z, h], {"expert": at * 2 + y},
+        )
+
+    def add_core(step, h):
+        at = nearest(z, step)
+        part_core(step, h).wait_recv()
+        for row in (1 - y, y):
+            mine = part[slot(step), h, c, row].astype(jnp.float32)
+            part[slot(step), h, c, row] = (
+                mine + from_core[at, h, row].astype(jnp.float32)
+            ).astype(jnp.bfloat16)
+        part_y(step, h).start()
+
+    def add_y(step, h):
+        at = nearest(z, step)
+        part_y(step, h).wait_recv()
+        mine = part[slot(step), h, c, y].astype(jnp.float32)
+        from_y[at, h] = (mine + from_y[at, h].astype(jnp.float32)).astype(jnp.bfloat16)
 
     first = place * held
+    span = width // HALVES
+    chain(1)
 
     def work(step, carry):
         at = nearest(z, step)
-
-        @pl.when(step < line - 1)
-        def _():
-            arrive_first(step + 1)
-
-        arrive_second(step)
+        arrive(step)
 
         @pl.when(step == 0)
         def _():
@@ -191,57 +218,86 @@
 
         lax.fori_loop(0, units // HID_TILE, hidden_tile, 0)
 
+        for far in range(2, line):
+            @pl.when(step == far - 2)
+            def _():
+                chain(far)
+
+        @pl.when(step == 0)
+        def _():
+            loads[2].wait()
+
+        @pl.when(step == 3)
+        def _():
+            for h in range(HALVES):
+                part_core(step - 2, h).wait_send()
+                part_y(step - 2, h).wait_send()
+
+        for h in range(HALVES):
+            def out_tile(j, carry):
+                inner = pl.ds(pl.multiple_of(j * OUT_TILE, OUT_TILE), OUT_TILE)
+                cols = pl.ds(pl.multiple_of(h * span + j * OUT_TILE, OUT_TILE), OUT_TILE)
+                total = jnp.dot(hid[...], down[:, cols], preferred_element_type=jnp.float32)
+                part[slot(step), h, :, :, :, inner] = total.astype(jnp.bfloat16).reshape(
+                    2, 2, rows, OUT_TILE
+                )
+                return carry
+
+            lax.fori_loop(0, span // OUT_TILE, out_tile, 0)
+            part_core(step, h).start()
+            if h > 0:
+                @pl.when(step > 0)
+                def _():
+                    add_core(step, h - 1)
+
         @pl.when(step > 0)
         def _():
-            add_core(step - 1)
-
-        @pl.when(step == 0)
-        def _():
-            loads[2].wait()
+            add_core(step, HALVES - 1)
 
         @pl.when(step > 1)
         def _():
-            part_core(step - 2).wait_send()
-            part_y(step - 2).wait_send()
-
-        def out_tile(j, carry):
-            cols = pl.ds(pl.multiple_of(j * OUT_TILE, OUT_TILE), OUT_TILE)
-            total = jnp.dot(hid[...], down[:, cols], preferred_element_type=jnp.float32)
-            part[step % 2, :, :, :, cols] = total.astype(jnp.bfloat16).reshape(
-                2, 2, rows, OUT_TILE
-            )
-            return carry
-
-        lax.fori_loop(0, width // OUT_TILE, out_tile, 0)
-        part_core(step).start()
-
-        @pl.when(step > 0)
-        def _():
-            add_y(step - 1)
+            for h in range(HALVES):
+                add_y(step - 1, h)
+                part_z(step - 1, h).start()
 
         return carry
 
     lax.fori_loop(0, line, work, 0)
-    add_core(line - 1)
-    add_y(line - 1)
-
-    total = from_y[z].astype(jnp.float32)
-    for d in range(1, line):
-        at = nearest(z, d)
-        remote(from_y.at[at], from_z.at[at], pzs.at[d], pzr.at[at], to_y).wait_recv()
-        total += from_z[at].astype(jnp.float32)
-    out_ref[...] = total.astype(out_ref.dtype)
-
-    for d in range(1, line):
-        z_send(d).wait_send()
-        part_z(d).wait_send()
+    for h in range(HALVES):
+        add_core(0, h)
+    for h in range(HALVES):
+        add_y(line - 1, h)
+        part_z(line - 1, h).start()
+
+    for h in range(HALVES):
+        add_y(0, h)
+        total = from_y[z, h].astype(jnp.float32)
+        for d in range(1, line):
+            at = nearest(z, d)
+            remote(
+                from_y.at[at, h], from_z.at[at, h], pzs.at[d, h], pzr.at[at, h], to_y
+            ).wait_recv()
+            total += from_z[at, h].astype(jnp.float32)
+        out_ref[:, pl.ds(h * span, span)] = total.astype(out_ref.dtype)
+
     for at in range(line):
+        @pl.when((at <= z) & (z < line - 1))
+        def _():
+            z_hop(at, True).wait_send()
+
+        @pl.when((at >= z) & (z > 0))
+        def _():
+            z_hop(at, False).wait_send()
+
         y_send(at).wait_send()
         for row in range(2):
             c_send(at, row).wait_send()
-    for step in range(line - 2, line):
-        part_core(step).wait_send()
-        part_y(step).wait_send()
+    for h in range(HALVES):
+        for d in range(1, line):
+            part_z(d, h).wait_send()
+        for step in (0, 2, 3):
+            part_core(step, h).wait_send()
+            part_y(step, h).wait_send()
 
 
 def in_one_kernel(tokens, expert_ids, route_weights, gate_weight, up_weight, down_weight):
@@ -266,24 +322,24 @@
             pltpu.VMEM(flat, bf16),
             pltpu.VMEM(flat, bf16),
             pltpu.VMEM((4 * rows, units), bf16),
-            pltpu.VMEM((2, 2, 2, rows, width), bf16),
-            pltpu.VMEM((line, 2, rows, width), bf16),
-            pltpu.VMEM((line, rows, width), bf16),
-            pltpu.VMEM((line, rows, width), bf16),
+            pltpu.VMEM((3, HALVES, 2, 2, rows, width // HALVES), bf16),
+            pltpu.VMEM((line, HALVES, 2, rows, width // HALVES), bf16),
+            pltpu.VMEM((line, HALVES, rows, width // HALVES), bf16),
+            pltpu.VMEM((line, HALVES, rows, width // HALVES), bf16),
             dma((3,)),
             dma,
-            dma((line,)),
+            dma((line, 2)),
             dma((line,)),
             dma((line,)),
             dma((line,)),
             dma((line, 2)),
             dma((line, 2)),
-            dma((line,)),
-            dma((line,)),
-            dma((line,)),
-            dma((line,)),
-            dma((line,)),
-            dma((line,)),
+            dma((line, HALVES)),
+            dma((line, HALVES)),
+            dma((line, HALVES)),
+            dma((line, HALVES)),
+            dma((line, HALVES)),
+            dma((line, HALVES)),
         ],
         compiler_params=pltpu.CompilerParams(
             collective_id=0, has_side_effects=True, vmem_limit_bytes=63 * 1024 * 1024

time: 167 us -> 140 us (0.84)
  Pallas kernels: 162 us -> 135 us
    pallas_call x1, Pallas kernels: 162 us -> 135 us  [in_one_kernel(): pl.pallas_call(functools.partial(kernel, line, held), out_shape=jax.Shape...]
where the time goes in v2:
time: 140 us
  Pallas kernels  135 us (96%)
  local copies, waits for them, and re-layouts  4.62 us (3%)
    pallas_call x1, Pallas kernels, in_one_kernel(): pl.pallas_call(functools.partial(kernel, line, held), out_shape=jax.Shape...  135 us
    unnamed x3, local copies, waits for them, and re-layouts  4.62 us

profile of v2, /device:TPU:0, one launch (start us, length us, event | category | flops | bytes accessed | tf_op | source)
XLA Modules:
  0.0 139.6 jit_solution(760714379045000827)
XLA Ops:
  0.0 1.4 copy.7.ids_ref
  1.4 1.4 copy.8.route_ref
  2.8 135.0 %experts.1 = bf16[64,4096]{1,0:T(8,128)(2,1)} custom-call(bf16[64,4096]{1,0:T(8,128)(2,1)} %tokens_ref.1, s32[64,8]{1,0:T(8,128)} %copy.7.ids_ref, f32[64,8]{1,0:T(8,128)} %copy.8.route_ref, bf16[1536,4096]{1,0:T(8,128)(2,1)} %bitcast.3, bf16[1536,4096]{1,0:T(8,128)(2,1)} %bitcast.4, bf16[1536,4096]{1,0:T(8,128)(2,1)} %bitcast.5), custom_call_target="tpu_custom_call" | custom-call | flops 38654705664 | bytes 37748736 | tf_op jit(solution)/shard_map/experts/pallas_call | solution.py:314
  137.7 1.9 %copy.10 = bf16[64,4096]{1,0:T(8,128)(2,1)} copy(bf16[64,4096]{1,0:T(8,128)(2,1)} %experts.1) | data formatting | bytes 1048576

commit v3 on v2

--- a/solution.py
+++ b/solution.py
@@ -154,12 +154,36 @@
             pys.at[step, h], pyr.at[step, h], to_y,
         )
 
-    def part_z(step, h):
-        at = nearest(z, step)
+    middle = (z > 0) & (z < line - 1)
+
+    def sum_send(step, h, up_line):
+        at = nearest(z, step)
+        there = z + 1 if up_line else z - 1
+        place_there = at if up_line else at + (line - at) * (1 - (z - 1 - at + line - 1) // line)
         return remote(
-            from_y.at[at, h], from_z.at[z, h],
-            pzs.at[step, h], pzr.at[z, h], {"expert": at * 2 + y},
+            from_y.at[at, h], from_z.at[place_there, h],
+            pzs.at[step, h], pzr.at[place_there, h], {"expert": there * 2 + y},
         )
+
+    def sum_arrival(at, h):
+        return remote(from_y.at[z, h], from_z.at[at, h], pzs.at[0, h], pzr.at[at, h], to_y)
+
+    def pass_on(step, h):
+        at = nearest(z, step)
+
+        @pl.when(middle)
+        def _():
+            sum_arrival(at, h).wait_recv()
+            mine = from_y[at, h].astype(jnp.float32)
+            from_y[at, h] = (mine + from_z[at, h].astype(jnp.float32)).astype(jnp.bfloat16)
+
+        @pl.when(at > z)
+        def _():
+            sum_send(step, h, True).start()
+
+        @pl.when(at < z)
+        def _():
+            sum_send(step, h, False).start()
 
     def add_core(step, h):
         at = nearest(z, step)
@@ -258,27 +282,51 @@
         def _():
             for h in range(HALVES):
                 add_y(step - 1, h)
-                part_z(step - 1, h).start()
+
+                @pl.when(jnp.logical_not(middle))
+                def _():
+                    pass_on(step - 1, h)
 
         return carry
 
     lax.fori_loop(0, line, work, 0)
     for h in range(HALVES):
         add_core(0, h)
+    @pl.when(middle)
+    def _():
+        for h in range(HALVES):
+            pass_on(line - 2, h)
+
     for h in range(HALVES):
         add_y(line - 1, h)
-        part_z(line - 1, h).start()
+        pass_on(line - 1, h)
+
+    @pl.when(middle)
+    def _():
+        for h in range(HALVES):
+            pass_on(1, h)
 
     for h in range(HALVES):
         add_y(0, h)
-        total = from_y[z, h].astype(jnp.float32)
-        for d in range(1, line):
-            at = nearest(z, d)
-            remote(
-                from_y.at[at, h], from_z.at[at, h], pzs.at[d, h], pzr.at[at, h], to_y
-            ).wait_recv()
-            total += from_z[at, h].astype(jnp.float32)
-        out_ref[:, pl.ds(h * span, span)] = total.astype(out_ref.dtype)
+
+        def finish(slots):
+            total = from_y[z, h].astype(jnp.float32)
+            for at in slots:
+                sum_arrival(at, h).wait_recv()
+                total += from_z[at, h].astype(jnp.float32)
+            out_ref[:, pl.ds(h * span, span)] = total.astype(out_ref.dtype)
+
+        @pl.when(z == 0)
+        def _():
+            finish((line,))
+
+        @pl.when(middle)
+        def _():
+            finish((z, line))
+
+        @pl.when(z == line - 1)
+        def _():
+            finish((z,))
 
     for at in range(line):
         @pl.when((at <= z) & (z < line - 1))
@@ -294,7 +342,9 @@
             c_send(at, row).wait_send()
     for h in range(HALVES):
         for d in range(1, line):
-            part_z(d, h).wait_send()
+            remote(
+                from_y.at[z, h], from_z.at[z, h], pzs.at[d, h], pzr.at[z, h], to_y
+            ).wait_send()
         for step in (0, 2, 3):
             part_core(step, h).wait_send()
             part_y(step, h).wait_send()
@@ -325,7 +375,7 @@
             pltpu.VMEM((3, HALVES, 2, 2, rows, width // HALVES), bf16),
             pltpu.VMEM((line, HALVES, 2, rows, width // HALVES), bf16),
             pltpu.VMEM((line, HALVES, rows, width // HALVES), bf16),
-            pltpu.VMEM((line, HALVES, rows, width // HALVES), bf16),
+            pltpu.VMEM((line + 1, HALVES, rows, width // HALVES), bf16),
             dma((3,)),
             dma,
             dma((line, 2)),
@@ -339,7 +389,7 @@
             dma((line, HALVES)),
             dma((line, HALVES)),
             dma((line, HALVES)),
-            dma((line, HALVES)),
+            dma((line + 1, HALVES)),
         ],
         compiler_params=pltpu.CompilerParams(
             collective_id=0, has_side_effects=True, vmem_limit_bytes=63 * 1024 * 1024

time: 140 us -> 133 us (0.950)
  Pallas kernels: 135 us -> 128 us
    pallas_call x1, Pallas kernels: 135 us -> 128 us  [in_one_kernel(): pl.pallas_call(functools.partial(kernel, line, held), out_shape=jax.Shape...]
where the time goes in v3:
time: 133 us
  Pallas kernels  128 us (96%)
  local copies, waits for them, and re-layouts  4.62 us (3%)
    pallas_call x1, Pallas kernels, in_one_kernel(): pl.pallas_call(functools.partial(kernel, line, held), out_shape=jax.Shape...  128 us
    unnamed x3, local copies, waits for them, and re-layouts  4.62 us

profile of v3, /device:TPU:0, one launch (start us, length us, event | category | flops | bytes accessed | tf_op | source)
XLA Modules:
  0.0 132.6 jit_solution(17497792605728738641)
XLA Ops:
  0.0 1.4 %copy.7.ids_ref = s32[64,8]{1,0:T(8,128)} copy(s32[64,8]{0,1:T(8,128)} %param.7) | data formatting | bytes 4096 | tf_op args[1]
  1.4 1.4 %copy.8.route_ref = f32[64,8]{1,0:T(8,128)} copy(f32[64,8]{0,1:T(8,128)} %param.8) | data formatting | bytes 4096 | tf_op args[2]
  2.8 128.0 %experts.1 = bf16[64,4096]{1,0:T(8,128)(2,1)} custom-call(bf16[64,4096]{1,0:T(8,128)(2,1)} %tokens_ref.1, s32[64,8]{1,0:T(8,128)} %copy.7.ids_ref, f32[64,8]{1,0:T(8,128)} %copy.8.route_ref, bf16[1536,4096]{1,0:T(8,128)(2,1)} %bitcast.3, bf16[1536,4096]{1,0:T(8,128)(2,1)} %bitcast.4, bf16[1536,4096]{1,0:T(8,128)(2,1)} %bitcast.5), custom_call_target="tpu_custom_call" | custom-call | flops 38654705664 | bytes 37748736 | tf_op jit(solution)/shard_map/experts/pallas_call | solution.py:364
  130.7 1.9 %copy.10 = bf16[64,4096]{1,0:T(8,128)(2,1)} copy(bf16[64,4096]{1,0:T(8,128)(2,1)} %experts.1) | data formatting | bytes 1048576

commit v4 on v3

--- a/solution.py
+++ b/solution.py
@@ -11,7 +11,7 @@
 EXTRA = 128
 HID_TILE = 256
 OUT_TILE = 512
-HALVES = 2
+PIECES = 4
 
 
 def nearest(z, step):
@@ -202,7 +202,7 @@
         from_y[at, h] = (mine + from_y[at, h].astype(jnp.float32)).astype(jnp.bfloat16)
 
     first = place * held
-    span = width // HALVES
+    span = width // PIECES
     chain(1)
 
     def work(step, carry):
@@ -253,11 +253,11 @@
 
         @pl.when(step == 3)
         def _():
-            for h in range(HALVES):
+            for h in range(PIECES):
                 part_core(step - 2, h).wait_send()
                 part_y(step - 2, h).wait_send()
 
-        for h in range(HALVES):
+        for h in range(PIECES):
             def out_tile(j, carry):
                 inner = pl.ds(pl.multiple_of(j * OUT_TILE, OUT_TILE), OUT_TILE)
                 cols = pl.ds(pl.multiple_of(h * span + j * OUT_TILE, OUT_TILE), OUT_TILE)
@@ -276,11 +276,11 @@
 
         @pl.when(step > 0)
         def _():
-            add_core(step, HALVES - 1)
+            add_core(step, PIECES - 1)
 
         @pl.when(step > 1)
         def _():
-            for h in range(HALVES):
+            for h in range(PIECES):
                 add_y(step - 1, h)
 
                 @pl.when(jnp.logical_not(middle))
@@ -290,23 +290,23 @@
         return carry
 
     lax.fori_loop(0, line, work, 0)
-    for h in range(HALVES):
+    for h in range(PIECES):
         add_core(0, h)
     @pl.when(middle)
     def _():
-        for h in range(HALVES):
+        for h in range(PIECES):
             pass_on(line - 2, h)
 
-    for h in range(HALVES):
+    for h in range(PIECES):
         add_y(line - 1, h)
         pass_on(line - 1, h)
 
     @pl.when(middle)
     def _():
-        for h in range(HALVES):
+        for h in range(PIECES):
             pass_on(1, h)
 
-    for h in range(HALVES):
+    for h in range(PIECES):
         add_y(0, h)
 
         def finish(slots):
@@ -340,7 +340,7 @@
         y_send(at).wait_send()
         for row in range(2):
             c_send(at, row).wait_send()
-    for h in range(HALVES):
+    for h in range(PIECES):
         for d in range(1, line):
             remote(
                 from_y.at[z, h], from_z.at[z, h], pzs.at[d, h], pzr.at[z, h], to_y
@@ -372,10 +372,10 @@
             pltpu.VMEM(flat, bf16),
             pltpu.VMEM(flat, bf16),
             pltpu.VMEM((4 * rows, units), bf16),
-            pltpu.VMEM((3, HALVES, 2, 2, rows, width // HALVES), bf16),
-            pltpu.VMEM((line, HALVES, 2, rows, width // HALVES), bf16),
-            pltpu.VMEM((line, HALVES, rows, width // HALVES), bf16),
-            pltpu.VMEM((line + 1, HALVES, rows, width // HALVES), bf16),
+            pltpu.VMEM((3, PIECES, 2, 2, rows, width // PIECES), bf16),
+            pltpu.VMEM((line, PIECES, 2, rows, width // PIECES), bf16),
+            pltpu.VMEM((line, PIECES, rows, width // PIECES), bf16),
+            pltpu.VMEM((line + 1, PIECES, rows, width // PIECES), bf16),
             dma((3,)),
             dma,
             dma((line, 2)),
@@ -384,12 +384,12 @@
             dma((line,)),
             dma((line, 2)),
             dma((line, 2)),
-            dma((line, HALVES)),
-            dma((line, HALVES)),
-            dma((line, HALVES)),
-            dma((line, HALVES)),
-            dma((line, HALVES)),
-            dma((line + 1, HALVES)),
+            dma((line, PIECES)),
+            dma((line, PIECES)),
+            dma((line, PIECES)),
+            dma((line, PIECES)),
+            dma((line, PIECES)),
+            dma((line + 1, PIECES)),
         ],
         compiler_params=pltpu.CompilerParams(
             collective_id=0, has_side_effects=True, vmem_limit_bytes=63 * 1024 * 1024

time: 133 us -> 132 us (level)
  no operation moved by 1% of the time
where the time goes in v4:
time: 132 us; the launch traced here: 131 us
  Pallas kernels  127 us (96%)
  local copies, waits for them, and re-layouts  4.62 us (4%)
    pallas_call x1, Pallas kernels, in_one_kernel(): pl.pallas_call(functools.partial(kernel, line, held), out_shape=jax.Shape...  127 us
    unnamed x3, local copies, waits for them, and re-layouts  4.62 us

profile of v4, /device:TPU:0, one launch (start us, length us, event | category | flops | bytes accessed | tf_op | source)
XLA Modules:
  0.0 131.3 jit_solution(7189752901118666190)
XLA Ops:
  0.0 1.4 %copy.7.ids_ref = s32[64,8]{1,0:T(8,128)} copy(s32[64,8]{0,1:T(8,128)} %param.7) | data formatting | bytes 4096 | tf_op args[1]
  1.4 1.4 %copy.8.route_ref = f32[64,8]{1,0:T(8,128)} copy(f32[64,8]{0,1:T(8,128)} %param.8) | data formatting | bytes 4096 | tf_op args[2]
  2.8 126.7 %experts.1 = bf16[64,4096]{1,0:T(8,128)(2,1)} custom-call(bf16[64,4096]{1,0:T(8,128)(2,1)} %tokens_ref.1, s32[64,8]{1,0:T(8,128)} %copy.7.ids_ref, f32[64,8]{1,0:T(8,128)} %copy.8.route_ref, bf16[1536,4096]{1,0:T(8,128)(2,1)} %bitcast.3, bf16[1536,4096]{1,0:T(8,128)(2,1)} %bitcast.4, bf16[1536,4096]{1,0:T(8,128)(2,1)} %bitcast.5), custom_call_target="tpu_custom_call" | custom-call | flops 38654705664 | bytes 37748736 | tf_op jit(solution)/shard_map/experts/pallas_call | solution.py:364
  129.4 1.9 %copy.10 = bf16[64,4096]{1,0:T(8,128)(2,1)} copy(bf16[64,4096]{1,0:T(8,128)(2,1)} %experts.1) | data formatting | bytes 1048576
